TPU v7x, 32 devices: a whole 2x2x4 slice. The times are simulated.
32 devices in a mesh: dp: 8 (over z, y), mp: 4 (over x, core).
Axes of the slice: x: 2, y: 2, z: 4, core: 2. Of those that a mesh axis runs over, the one named last changes fastest.
Arguments:
- statistics: float32 [384, 256, 256], P(('dp', 'mp')), may hold values from -6 to 40, as said below
- gradient: float32 [192, 256, 256], P('dp', 'mp'), may hold values from -6 to 6
- root_table: int32 [4, 96], P('mp'), may hold values from 0 to 7, as said below
Outputs:
- root_store: float32 [768, 256, 256], P(('dp', 'mp'))
- update: float32 [192, 256, 256], P('dp', 'mp')
Inputs may be any that keep to these rules, and one draw needn't show every extreme that they name: `statistics`: every block is symmetric and positive definite. `root_table`: in each row no worker is named more than 24 times and some worker exactly 24 times; the 12 entries of one dp index name no worker more than 3 times, and in each row some dp index names one worker exactly 3 times.
All inputs are finite; a program needn't handle non-finite values.
Results may differ from a plain program's by a relative error of at most 0.00022.
Values sent between devices are 32-bit elements; how exact they have to be, the bound alone decides.
A program may use at most 128 MiB of HBM per device.

v0:
```python
import functools

import jax
import jax.numpy as jnp
from jax import lax
from jax.experimental import pallas as pl
from jax.experimental.pallas import tpu as pltpu
from jax.sharding import PartitionSpec as P

MESH = pl.DeviceIdType.MESH
F32 = jnp.float32
BF16 = jnp.bfloat16


def one_pass(left, right):
    return jnp.dot(left.astype(BF16), right.astype(BF16), preferred_element_type=F32)


def halves(value):
    high = value.astype(BF16)
    return high, (value - high.astype(F32)).astype(BF16)


def three_pass(left, right):
    left_high, left_low = halves(left)
    right_high, right_low = halves(right)
    dot = functools.partial(jnp.dot, preferred_element_type=F32)
    return dot(left_high, right_high) + (dot(left_high, right_low) + dot(left_low, right_high))


def inverse_root(stat, eye_mask):
    scale = jnp.sqrt(jnp.sum(stat * stat, keepdims=True) + 1e-06)
    quarter = 1.0 / jnp.sqrt(jnp.sqrt(scale))
    x = stat * (-0.25 / scale)
    c = 1.5625
    xx = one_pass(x, x)
    a = 2.5 * x + xx
    b = 3.125 * a + one_pass(a, a)
    d = 1.25 * x + xx
    y = 1.25 * x + (c * c) * d + one_pass(b, d)
    z = (2 * c) * y + one_pass(y, y)
    w = (2 * c * c) * z + one_pass(z, z)
    t = c * x + one_pass(x, y)
    e = 1.25 * y + (c**4) * t + three_pass(w, t)
    return quarter * jnp.where(eye_mask, e + 1.25 * c, e)


def shifts(count):
    return sorted(range(1, count), key=lambda k: abs(k - count / 2))


def spread_kernel(
    dp_count,
    mp_count,
    per_peer,
    group,
    table_ref,
    stat_ref,
    grad_ref,
    recv_ref,
    back_ref,
    roots,
    packed,
    corner,
    staged,
    whole,
    result,
    grad_send,
    grad_recv,
    back_send,
    back_recv,
    out_send,
    out_recv,
    local_sem,
):
    dp_me = lax.axis_index("dp")
    mp_me = lax.axis_index("mp")
    factors, width = stat_ref.shape[0], stat_ref.shape[1]
    half = width // 2
    pairs = factors // 2
    rows = width // mp_count
    barrier = pltpu.get_barrier_semaphore()
    for k in range(1, dp_count):
        pl.semaphore_signal(
            barrier, inc=1, device_id=(lax.rem(dp_me + k, dp_count), mp_me), device_id_type=MESH
        )
    for j in range(1, mp_count):
        pl.semaphore_signal(
            barrier, inc=1, device_id=(dp_me, lax.rem(mp_me + j, mp_count)), device_id_type=MESH
        )
    pl.semaphore_wait(barrier, dp_count + mp_count - 2)

    my_rows = pl.ds(pl.multiple_of(mp_me * rows, rows), rows)
    grad_copies = []
    for j in range(1, mp_count):
        peer = lax.rem(mp_me + j, mp_count)
        copy = pltpu.make_async_remote_copy(
            src_ref=grad_ref.at[pl.ds(peer * pairs, pairs)],
            dst_ref=whole.at[:, my_rows, :],
            send_sem=grad_send.at[j - 1],
            recv_sem=grad_recv.at[j - 1],
            device_id=(dp_me, peer),
            device_id_type=MESH,
        )
        copy.start()
        grad_copies.append(copy)
    own_grad = pltpu.make_async_copy(
        grad_ref.at[pl.ds(mp_me * pairs, pairs)], whole.at[:, my_rows, :], local_sem.at[0]
    )
    own_grad.start()

    down = lax.broadcasted_iota(jnp.int32, (half, half), 0)
    across = lax.broadcasted_iota(jnp.int32, (half, half), 1)
    eye_mask = lax.broadcasted_iota(jnp.int32, (width, width), 0) == lax.broadcasted_iota(
        jnp.int32, (width, width), 1
    )

    def make_roots(step, carry):
        for i in range(group):
            f = step * group + i
            root = inverse_root(stat_ref[f], eye_mask)
            roots[f] = root
            low = root[half:, half:]
            packed[f, :half, :] = root[half:, :half]
            packed[f, half:, :] = jnp.where(down >= across, root[:half, :half], low)
            diagonal = jnp.sum(jnp.where(down == across, low, 0.0), axis=0, keepdims=True)
            corner[f] = jnp.broadcast_to(diagonal, (8, half))
        return carry

    lax.fori_loop(0, factors // group, make_roots, 0)

    body = per_peer * width
    copies = []
    for k in shifts(dp_count) + [0]:
        peer = lax.rem(dp_me + k, dp_count)
        picks = [jnp.int32(0)] * per_peer
        filled = jnp.int32(0)
        base = dp_me * factors
        for f in range(factors):
            hit = table_ref[0, base + f] == peer
            for c in range(per_peer):
                picks[c] = jnp.where(jnp.logical_and(hit, filled == c), f, picks[c])
            filled = filled + hit.astype(jnp.int32)
        for c in range(per_peer):
            staged[k, c * width : (c + 1) * width, :] = packed[picks[c]]
            staged[k, body + 8 * c : body + 8 * c + 8, :] = corner[picks[c]]
        if k:
            copy = pltpu.make_async_remote_copy(
                src_ref=staged.at[k],
                dst_ref=recv_ref.at[dp_me],
                send_sem=out_send.at[k - 1],
                recv_sem=out_recv.at[k - 1],
                device_id=(peer, mp_me),
                device_id_type=MESH,
            )
            copy.start()
            copies.append(copy)
    own_roots = pltpu.make_async_copy(staged.at[0], recv_ref.at[dp_me], local_sem.at[1])
    own_roots.start()

    own_grad.wait()
    for copy in grad_copies:
        copy.wait()

    def apply(m, carry):
        left = three_pass(roots[2 * m], whole[m])
        result[m] = three_pass(left, roots[2 * m + 1])
        return carry

    lax.fori_loop(0, pairs, apply, 0)

    back_copies = []
    for j in range(1, mp_count):
        peer = lax.rem(mp_me + j, mp_count)
        copy = pltpu.make_async_remote_copy(
            src_ref=result.at[:, pl.ds(pl.multiple_of(peer * rows, rows), rows), :],
            dst_ref=back_ref.at[pl.ds(mp_me * pairs, pairs)],
            send_sem=back_send.at[j - 1],
            recv_sem=back_recv.at[j - 1],
            device_id=(dp_me, peer),
            device_id_type=MESH,
        )
        copy.start()
        back_copies.append(copy)
    own_back = pltpu.make_async_copy(
        result.at[:, my_rows, :], back_ref.at[pl.ds(mp_me * pairs, pairs)], local_sem.at[2]
    )
    own_back.start()
    own_back.wait()
    own_roots.wait()
    for copy in back_copies:
        copy.wait()
    for copy in copies:
        copy.wait()


def store_kernel(
    dp_count,
    per_peer,
    factors,
    per_step,
    table_ref,
    recv_ref,
    back_ref,
    store_ref,
    update_ref,
    sources,
    places,
    update_sem,
):
    step = pl.program_id(0)
    me = lax.axis_index("dp")
    half = store_ref.shape[2] // 2
    capacity = 2 * factors
    update_copy = pltpu.make_async_copy(back_ref, update_ref, update_sem)

    @pl.when(step == 0)
    def _():
        update_copy.start()
        for c in range(capacity + 1):
            sources[c] = -1
            places[c] = 0

        def from_source(source, slot):
            place = jnp.int32(0)
            for f in range(factors):
                hit = (table_ref[0, source * factors + f] == me).astype(jnp.int32)
                at = jnp.where(hit == 1, jnp.minimum(slot, capacity), capacity)
                sources[at] = source
                places[at] = place
                place = jnp.minimum(place + hit, per_peer - 1)
                slot = slot + hit
            return slot

        lax.fori_loop(0, dp_count, from_source, jnp.int32(0))

    down = lax.broadcasted_iota(jnp.int32, (half, half), 0)
    across = lax.broadcasted_iota(jnp.int32, (half, half), 1)
    body = per_peer * 2 * half
    for i in range(per_step):
        slot = step * per_step + i
        taken = sources[slot] >= 0
        source = jnp.maximum(sources[slot], 0)
        place = places[slot]
        first = pl.multiple_of(place * 2 * half, 2 * half)
        cross = recv_ref[source, pl.ds(first, half), :]
        mixed = recv_ref[source, pl.ds(pl.multiple_of(first + half, half), half), :]
        corner = recv_ref[source, pl.ds(pl.multiple_of(body + 8 * place, 8), 8), :][:1]
        cross = jnp.where(taken, cross, 0.0)
        mixed = jnp.where(taken, mixed, 0.0)
        corner = jnp.where(taken, corner, 0.0)
        turned = mixed.T
        store_ref[i, :half, :half] = jnp.where(down >= across, mixed, turned)
        store_ref[i, :half, half:] = cross.T
        store_ref[i, half:, :half] = cross
        store_ref[i, half:, half:] = jnp.where(
            down < across, mixed, jnp.where(down == across, corner, turned)
        )

    @pl.when(step == pl.num_programs(0) - 1)
    def _():
        update_copy.wait()


def on_device(statistics, gradient, root_table):
    dp_count = lax.axis_size("dp")
    mp_count = lax.axis_size("mp")
    factors, width = statistics.shape[0], statistics.shape[1]
    half, pairs = width // 2, factors // 2
    per_peer = (2 * factors + dp_count - 1) // dp_count
    group = 2 if factors % 2 == 0 else 1
    length = per_peer * (width + 8)
    table_spec = pl.BlockSpec(memory_space=pltpu.SMEM)
    any_spec = pl.BlockSpec(memory_space=pl.ANY)
    vmem_spec = pl.BlockSpec(memory_space=pltpu.VMEM)
    received, back = pl.pallas_call(
        functools.partial(spread_kernel, dp_count, mp_count, per_peer, group),
        out_shape=(
            jax.ShapeDtypeStruct((dp_count, length, half), F32),
            jax.ShapeDtypeStruct(gradient.shape, F32),
        ),
        in_specs=[table_spec, vmem_spec, any_spec],
        out_specs=(any_spec, any_spec),
        scratch_shapes=[
            pltpu.VMEM((factors, width, width), F32),
            pltpu.VMEM((factors, width, half), F32),
            pltpu.VMEM((factors, 8, half), F32),
            pltpu.VMEM((dp_count, length, half), F32),
            pltpu.VMEM((pairs, width, width), F32),
            pltpu.VMEM((pairs, width, width), F32),
            pltpu.SemaphoreType.DMA((mp_count - 1,)),
            pltpu.SemaphoreType.DMA((mp_count - 1,)),
            pltpu.SemaphoreType.DMA((mp_count - 1,)),
            pltpu.SemaphoreType.DMA((mp_count - 1,)),
            pltpu.SemaphoreType.DMA((dp_count - 1,)),
            pltpu.SemaphoreType.DMA((dp_count - 1,)),
            pltpu.SemaphoreType.DMA((3,)),
        ],
        compiler_params=pltpu.CompilerParams(
            collective_id=0, has_side_effects=True, vmem_limit_bytes=48 * 2**20
        ),
    )(root_table, statistics, gradient)
    per_step = 2
    capacity = 2 * factors
    return pl.pallas_call(
        functools.partial(store_kernel, dp_count, per_peer, factors, per_step),
        grid=(capacity // per_step,),
        out_shape=(
            jax.ShapeDtypeStruct((capacity, width, width), F32),
            jax.ShapeDtypeStruct(gradient.shape, F32),
        ),
        in_specs=[table_spec, vmem_spec, any_spec],
        out_specs=(pl.BlockSpec((per_step, width, width), lambda s: (s, 0, 0)), any_spec),
        scratch_shapes=[
            pltpu.SMEM((capacity + 1,), jnp.int32),
            pltpu.SMEM((capacity + 1,), jnp.int32),
            pltpu.SemaphoreType.DMA,
        ],
        compiler_params=pltpu.CompilerParams(vmem_limit_bytes=32 * 2**20),
    )(root_table, received, back)


def solution(mesh):
    return jax.shard_map(
        on_device,
        mesh=mesh,
        in_specs=(P(("dp", "mp"), None, None), P("dp", "mp", None), P("mp", None)),
        out_specs=(P(("dp", "mp"), None, None), P("dp", "mp", None)),
        check_vma=False,
    )
```

profile of v0, /device:TPU:8, one launch (start us, length us, event | category | flops | bytes accessed | tf_op | source)
XLA Modules:
  0.0 99.0 jit_solution(62039704144882255)
XLA Ops:
  0.6 0.0 copy-start.1
  0.6 1.4 %copy-done.1 = f32[24,64,256]{2,1,0:T(8,128)S(1)} copy-done((f32[24,64,256]{2,1,0:T(8,128)S(1)}, f32[24,64,256]{2,1,0:T(8,128)}, u32[]{:S(2)}) %copy-start.1) | copy-done | bytes 1572888
  2.0 0.0 copy-start.2
  2.0 0.7 copy-done.2
  2.7 87.4 %shard_map.50 = (f32[8,792,128]{2,1,0:T(8,128)}, f32[24,64,256]{2,1,0:T(8,128)S(1)}) custom-call(s32[1,96]{1,0:T(1,128)S(1)} %copy-done.2, f32[12,256,256]{2,1,0:T(8,128)} %stat_ref.1, f32[24,64,256]{2,1,0:T(8,128)S(1)} %copy-done.1), custom_call_target="tpu_custom_call" | custom-call | tf_op jit(solution)/shard_map/pallas_call | solution.py:276
  90.1 0.0 copy-start
  90.2 1.9 %copy-done = f32[8,792,128]{2,1,0:T(8,128)S(1)} copy-done((f32[8,792,128]{2,1,0:T(8,128)S(1)}, f32[8,792,128]{2,1,0:T(8,128)}, u32[]{:S(2)}) %copy-start) | copy-done | bytes 3244056
  92.1 6.9 %shard_map.51 = (f32[24,256,256]{2,1,0:T(8,128)}, f32[24,64,256]{2,1,0:T(8,128)}) custom-call(s32[1,96]{1,0:T(1,128)S(1)} %copy-done.2, f32[8,792,128]{2,1,0:T(8,128)S(1)} %copy-done, f32[24,64,256]{2,1,0:T(8,128)S(1)} %get-tuple-element.5.back_ref), custom_call_target="tpu_custom_call" | custom-call | tf_op jit(solution)/shard_map/pallas_call | solution.py:305
Async XLA Ops:
  0.6 1.4 %copy-start.1 = (f32[24,64,256]{2,1,0:T(8,128)S(1)}, f32[24,64,256]{2,1,0:T(8,128)}, u32[]{:S(2)}) copy-start(f32[24,64,256]{2,1,0:T(8,128)} %grad_ref.1) | copy-start | bytes 4718596
  2.0 0.7 copy-start.2
  90.1 1.9 %copy-start = (f32[8,792,128]{2,1,0:T(8,128)S(1)}, f32[8,792,128]{2,1,0:T(8,128)}, u32[]{:S(2)}) copy-start(f32[8,792,128]{2,1,0:T(8,128)} %get-tuple-element.4.recv_ref) | copy-start | bytes 9732100
where the time goes:
time: 100 us; the launch traced here: 99 us
  Pallas kernels  94.4 us (94%)
  local copies, waits for them, and re-layouts  3.97 us (4%)
    pallas_call x1, Pallas kernels, on_device(): pl.pallas_call(functools.partial(spread_kernel, dp_count, mp_count, per_p...  87.4 us
    pallas_call x1, Pallas kernels, on_device(): pl.pallas_call(functools.partial(store_kernel, dp_count, per_peer, factor...  6.91 us
    unnamed x6, local copies, waits for them, and re-layouts  3.97 us

commit v1 on v0

v1 whole, which is shorter than its diff:
```python
import functools

import jax
import jax.numpy as jnp
from jax import lax
from jax.experimental import pallas as pl
from jax.experimental.pallas import tpu as pltpu
from jax.sharding import PartitionSpec as P

MESH = pl.DeviceIdType.MESH
F32 = jnp.float32
BF16 = jnp.bfloat16


def one_pass(left, right):
    return jnp.dot(left.astype(BF16), right.astype(BF16), preferred_element_type=F32)


def halves(value):
    high = value.astype(BF16)
    return high, (value - high.astype(F32)).astype(BF16)


def three_pass(left, right):
    left_high, left_low = halves(left)
    right_high, right_low = halves(right)
    dot = functools.partial(jnp.dot, preferred_element_type=F32)
    return dot(left_high, right_high) + (dot(left_high, right_low) + dot(left_low, right_high))


def inverse_root(stat, eye_mask):
    scale = jnp.sqrt(jnp.sum(stat * stat, keepdims=True) + 1e-06)
    quarter = 1.0 / jnp.sqrt(jnp.sqrt(scale))
    x = stat * (-0.25 / scale)
    c = 1.5625
    xx = one_pass(x, x)
    a = 2.5 * x + xx
    b = 3.125 * a + one_pass(a, a)
    d = 1.25 * x + xx
    y = 1.25 * x + (c * c) * d + one_pass(b, d)
    z = (2 * c) * y + one_pass(y, y)
    w = (2 * c * c) * z + one_pass(z, z)
    t = c * x + one_pass(x, y)
    e = 1.25 * y + (c**4) * t + three_pass(w, t)
    return quarter * jnp.where(eye_mask, e + 1.25 * c, e)


def flipped(me, mask, count):
    peer = me
    bit = 1
    while bit < count:
        peer = peer + (mask // bit % 2) * (1 - 2 * (me // bit % 2)) * bit
        bit *= 2
    return peer


def spread_kernel(
    dp_count,
    mp_count,
    per_peer,
    table_ref,
    stat_ref,
    grad_ref,
    recv_ref,
    back_ref,
    codes_ref,
    stats,
    roots,
    packed,
    corner,
    staged,
    whole,
    result,
    order,
    position,
    bases,
    grad_send,
    grad_recv,
    back_send,
    back_recv,
    out_send,
    out_recv,
    local_sem,
):
    dp_me = lax.axis_index("dp")
    mp_me = lax.axis_index("mp")
    factors, width = stats.shape[0], stats.shape[1]
    half = width // 2
    pairs = factors // 2
    rows = width // mp_count
    stat_copy = pltpu.make_async_copy(stat_ref, stats, local_sem.at[3])
    stat_copy.start()
    my_rows = pl.ds(pl.multiple_of(mp_me * rows, rows), rows)
    own_grad = pltpu.make_async_copy(
        grad_ref.at[pl.ds(mp_me * pairs, pairs)], whole.at[:, my_rows, :], local_sem.at[0]
    )
    own_grad.start()
    barrier = pltpu.get_barrier_semaphore()
    for k in range(1, dp_count):
        pl.semaphore_signal(
            barrier, inc=1, device_id=(lax.rem(dp_me + k, dp_count), mp_me), device_id_type=MESH
        )
    for j in range(1, mp_count):
        pl.semaphore_signal(
            barrier, inc=1, device_id=(dp_me, lax.rem(mp_me + j, mp_count)), device_id_type=MESH
        )

    targets = [table_ref[0, dp_me * factors + f] for f in range(factors)]
    places = [jnp.int32(0)] * factors
    running = jnp.int32(0)
    for s in range(dp_count):
        peer = flipped(dp_me, dp_count - 1 - s, dp_count)
        bases[s] = running
        for f in range(factors):
            hit = targets[f] == peer
            places[f] = jnp.where(hit, running, places[f])
            running = running + hit.astype(jnp.int32)
    for f in range(factors):
        position[f] = places[f]
    for i in range(factors):
        which = jnp.int32(0)
        for f in range(factors):
            which = jnp.where(places[f] == i, f, which)
        order[i] = which

    pl.semaphore_wait(barrier, dp_count + mp_count - 2)
    grad_copies = []
    for j in range(1, mp_count):
        peer = lax.rem(mp_me + j, mp_count)
        copy = pltpu.make_async_remote_copy(
            src_ref=grad_ref.at[pl.ds(peer * pairs, pairs)],
            dst_ref=whole.at[:, my_rows, :],
            send_sem=grad_send.at[j - 1],
            recv_sem=grad_recv.at[j - 1],
            device_id=(dp_me, peer),
            device_id_type=MESH,
        )
        copy.start()
        grad_copies.append(copy)

    down = lax.broadcasted_iota(jnp.int32, (half, half), 0)
    across = lax.broadcasted_iota(jnp.int32, (half, half), 1)
    eye_mask = lax.broadcasted_iota(jnp.int32, (width, width), 0) == lax.broadcasted_iota(
        jnp.int32, (width, width), 1
    )
    body = per_peer * width
    tail = staged.shape[1] - body
    tail_row = lax.broadcasted_iota(jnp.int32, (tail, half), 0)

    def stage(s):
        corners = jnp.zeros((tail, half), F32)
        for c in range(per_peer):
            at = jnp.minimum(bases[s] + c, factors - 1)
            staged[s, c * width : (c + 1) * width, :] = packed[at]
            corners = jnp.where(tail_row == c, corner[at][:1], corners)
        staged[s, body:, :] = corners

    def send(s):
        return pltpu.make_async_remote_copy(
            src_ref=staged.at[s],
            dst_ref=recv_ref.at[dp_me],
            send_sem=out_send.at[s],
            recv_sem=out_recv.at[s],
            device_id=(flipped(dp_me, dp_count - 1 - s, dp_count), mp_me),
            device_id_type=MESH,
        )

    stat_copy.wait()
    steps = factors // per_peer

    def make_roots(step, carry):
        for i in range(per_peer):
            f = step * per_peer + i
            root = inverse_root(stats[order[f]], eye_mask)
            roots[f] = root
            low = root[half:, half:]
            packed[f, :half, :] = root[half:, :half]
            packed[f, half:, :] = jnp.where(down >= across, root[:half, :half], low)
            diagonal = jnp.sum(jnp.where(down == across, low, 0.0), axis=0, keepdims=True)
            corner[f] = jnp.broadcast_to(diagonal, (8, half))
        stage(step)
        send(step).start()
        return carry

    def send_rest(s, carry):
        stage(s)
        send(s).start()
        return carry

    for f in range(factors):
        packed[f] = jnp.zeros((width, half), F32)
        corner[f] = jnp.zeros((8, half), F32)
    lax.fori_loop(0, steps, make_roots, 0)
    lax.fori_loop(steps, dp_count - 1, send_rest, 0)
    stage(dp_count - 1)
    own_roots = pltpu.make_async_copy(
        staged.at[dp_count - 1], recv_ref.at[dp_me], local_sem.at[1]
    )
    own_roots.start()

    own_grad.wait()
    for copy in grad_copies:
        copy.wait()

    def apply(m, carry):
        left = three_pass(roots[position[2 * m]], whole[m])
        result[m] = three_pass(left, roots[position[2 * m + 1]])
        return carry

    lax.fori_loop(0, pairs, apply, 0)

    back_copies = []
    for j in range(1, mp_count):
        peer = lax.rem(mp_me + j, mp_count)
        copy = pltpu.make_async_remote_copy(
            src_ref=result.at[:, pl.ds(pl.multiple_of(peer * rows, rows), rows), :],
            dst_ref=back_ref.at[pl.ds(mp_me * pairs, pairs)],
            send_sem=back_send.at[j - 1],
            recv_sem=back_recv.at[j - 1],
            device_id=(dp_me, peer),
            device_id_type=MESH,
        )
        copy.start()
        back_copies.append(copy)
    own_back = pltpu.make_async_copy(
        result.at[:, my_rows, :], back_ref.at[pl.ds(mp_me * pairs, pairs)], local_sem.at[2]
    )
    own_back.start()

    def find(c, carry):
        def from_source(source, state):
            slot, code = state
            place = source * per_peer
            for f in range(factors):
                hit = table_ref[0, source * factors + f] == dp_me
                code = jnp.where(jnp.logical_and(hit, slot == c), place, code)
                slot = slot + hit.astype(jnp.int32)
                place = place + hit.astype(jnp.int32)
            return slot, code

        codes_ref[0, c] = lax.fori_loop(
            0, dp_count, from_source, (jnp.int32(0), jnp.int32(-1))
        )[1]
        return carry

    lax.fori_loop(0, 2 * factors, find, 0)

    own_back.wait()
    own_roots.wait()
    for copy in back_copies:
        copy.wait()

    def finish(s, carry):
        send(s).wait()
        return carry

    lax.fori_loop(0, dp_count - 1, finish, 0)


def store_kernel(
    per_peer,
    per_step,
    codes_ref,
    recv_ref,
    back_ref,
    store_ref,
    update_ref,
    update_sem,
):
    step = pl.program_id(0)
    half = store_ref.shape[2] // 2
    update_copy = pltpu.make_async_copy(back_ref, update_ref, update_sem)

    @pl.when(step == 0)
    def _():
        update_copy.start()

    down = lax.broadcasted_iota(jnp.int32, (half, half), 0)
    across = lax.broadcasted_iota(jnp.int32, (half, half), 1)
    body = per_peer * 2 * half
    tail = recv_ref.shape[1] - body
    tail_row = lax.broadcasted_iota(jnp.int32, (tail, half), 0)
    for i in range(per_step):
        code = codes_ref[0, step * per_step + i]
        taken = code >= 0
        source = jnp.maximum(code, 0) // per_peer
        place = jnp.maximum(code, 0) % per_peer
        first = pl.multiple_of(place * 2 * half, 2 * half)
        cross = recv_ref[source, pl.ds(first, half), :]
        mixed = recv_ref[source, pl.ds(pl.multiple_of(first + half, half), half), :]
        corners = recv_ref[source, pl.ds(body, tail), :]
        cross = jnp.where(taken, cross, 0.0)
        mixed = jnp.where(taken, mixed, 0.0)
        chosen = jnp.logical_and(tail_row == place, taken)
        corner = jnp.sum(jnp.where(chosen, corners, 0.0), axis=0, keepdims=True)
        turned = mixed.T
        store_ref[i, :half, :half] = jnp.where(down >= across, mixed, turned)
        store_ref[i, :half, half:] = cross.T
        store_ref[i, half:, :half] = cross
        store_ref[i, half:, half:] = jnp.where(
            down < across, mixed, jnp.where(down == across, corner, turned)
        )

    @pl.when(step == pl.num_programs(0) - 1)
    def _():
        update_copy.wait()


def on_device(statistics, gradient, root_table):
    dp_count = lax.axis_size("dp")
    mp_count = lax.axis_size("mp")
    factors, width = statistics.shape[0], statistics.shape[1]
    half, pairs = width // 2, factors // 2
    capacity = 2 * factors
    per_peer = (capacity + dp_count - 1) // dp_count
    length = per_peer * width + (per_peer + 7) // 8 * 8
    smem_spec = pl.BlockSpec(memory_space=pltpu.SMEM)
    any_spec = pl.BlockSpec(memory_space=pl.ANY)
    vmem_spec = pl.BlockSpec(memory_space=pltpu.VMEM)
    hbm_spec = pl.BlockSpec(memory_space=pltpu.HBM)
    received, back, codes = pl.pallas_call(
        functools.partial(spread_kernel, dp_count, mp_count, per_peer),
        out_shape=(
            jax.ShapeDtypeStruct((dp_count, length, half), F32),
            jax.ShapeDtypeStruct(gradient.shape, F32),
            jax.ShapeDtypeStruct((1, capacity), jnp.int32),
        ),
        in_specs=[smem_spec, hbm_spec, hbm_spec],
        out_specs=(any_spec, any_spec, smem_spec),
        scratch_shapes=[
            pltpu.VMEM((factors, width, width), F32),
            pltpu.VMEM((factors, width, width), F32),
            pltpu.VMEM((factors, width, half), F32),
            pltpu.VMEM((factors, 8, half), F32),
            pltpu.VMEM((dp_count, length, half), F32),
            pltpu.VMEM((pairs, width, width), F32),
            pltpu.VMEM((pairs, width, width), F32),
            pltpu.SMEM((factors,), jnp.int32),
            pltpu.SMEM((factors,), jnp.int32),
            pltpu.SMEM((dp_count,), jnp.int32),
            pltpu.SemaphoreType.DMA((mp_count - 1,)),
            pltpu.SemaphoreType.DMA((mp_count - 1,)),
            pltpu.SemaphoreType.DMA((mp_count - 1,)),
            pltpu.SemaphoreType.DMA((mp_count - 1,)),
            pltpu.SemaphoreType.DMA((dp_count - 1,)),
            pltpu.SemaphoreType.DMA((dp_count - 1,)),
            pltpu.SemaphoreType.DMA((4,)),
        ],
        compiler_params=pltpu.CompilerParams(
            collective_id=0, has_side_effects=True, vmem_limit_bytes=28 * 2**20
        ),
    )(root_table, statistics, gradient)
    per_step = 2
    return pl.pallas_call(
        functools.partial(store_kernel, per_peer, per_step),
        grid=(capacity // per_step,),
        out_shape=(
            jax.ShapeDtypeStruct((capacity, width, width), F32),
            jax.ShapeDtypeStruct(gradient.shape, F32),
        ),
        in_specs=[smem_spec, vmem_spec, any_spec],
        out_specs=(pl.BlockSpec((per_step, width, width), lambda s: (s, 0, 0)), any_spec),
        scratch_shapes=[pltpu.SemaphoreType.DMA],
        compiler_params=pltpu.CompilerParams(vmem_limit_bytes=16 * 2**20),
    )(codes, received, back)


def solution(mesh):
    return jax.shard_map(
        on_device,
        mesh=mesh,
        in_specs=(P(("dp", "mp"), None, None), P("dp", "mp", None), P("mp", None)),
        out_specs=(P(("dp", "mp"), None, None), P("dp", "mp", None)),
        check_vma=False,
    )
```

time: 100 us -> 96.6 us (0.966)
  the two profiles are of different devices: /device:TPU:8 before, /device:TPU:0 now
where the time goes in v1:
time: 96.6 us; the launch traced here: 96.4 us
  Pallas kernels  91.8 us (95%)
  local copies, waits for them, and re-layouts  3.94 us (4%)
    pallas_call x1, Pallas kernels, on_device(): pl.pallas_call(functools.partial(spread_kernel, dp_count, mp_count, per_p...  85 us
    pallas_call x1, Pallas kernels, on_device(): pl.pallas_call(functools.partial(store_kernel, per_peer, per_step), grid=...  6.83 us
    unnamed x6, local copies, waits for them, and re-layouts  3.94 us

profile of v1, /device:TPU:0, one launch (start us, length us, event | category | flops | bytes accessed | tf_op | source)
XLA Modules:
  0.0 96.4 jit_solution(5217956203181946025)
XLA Ops:
  0.6 0.0 copy-start
  0.6 1.9 %copy-done = f32[12,256,256]{2,1,0:T(8,128)S(1)} copy-done((f32[12,256,256]{2,1,0:T(8,128)S(1)}, f32[12,256,256]{2,1,0:T(8,128)}, u32[]{:S(2)}) %copy-start) | copy-done | bytes 3145752
  2.5 0.0 copy-start.1
  2.5 1.4 %copy-done.1 = f32[24,64,256]{2,1,0:T(8,128)S(1)} copy-done((f32[24,64,256]{2,1,0:T(8,128)S(1)}, f32[24,64,256]{2,1,0:T(8,128)}, u32[]{:S(2)}) %copy-start.1) | copy-done | bytes 1572888
  3.9 0.0 copy-start.2
  3.9 0.7 copy-done.2
  4.6 85.0 %shard_map.50 = (f32[8,776,128]{2,1,0:T(8,128)S(1)}, f32[24,64,256]{2,1,0:T(8,128)S(1)}, s32[1,24]{1,0:T(1,128)S(1)}) custom-call(s32[1,96]{1,0:T(1,128)S(1)} %copy-done.2, f32[12,256,256]{2,1,0:T(8,128)S(1)} %copy-done, f32[24,64,256]{2,1,0:T(8,128)S(1)} %copy-done.1), custom_call_target="tpu_custom_call" | custom-call | tf_op jit(solution)/shard_map/pallas_call | solution.py:321
  89.6 6.8 %shard_map.51 = (f32[24,256,256]{2,1,0:T(8,128)}, f32[24,64,256]{2,1,0:T(8,128)}) custom-call(s32[1,24]{1,0:T(1,128)S(1)} %get-tuple-element.5.codes_ref, f32[8,776,128]{2,1,0:T(8,128)S(1)} %get-tuple-element.6.recv_ref, f32[24,64,256]{2,1,0:T(8,128)S(1)} %get-tuple-element.7.back_ref), custom_call_target="tpu_custom_call" | custom-call | tf_op jit(solution)/shard_map/pallas_call | solution.py:354
Async XLA Ops:
  0.6 1.9 %copy-start = (f32[12,256,256]{2,1,0:T(8,128)S(1)}, f32[12,256,256]{2,1,0:T(8,128)}, u32[]{:S(2)}) copy-start(f32[12,256,256]{2,1,0:T(8,128)} %stat_ref.1) | copy-start | bytes 9437188
  2.5 1.4 %copy-start.1 = (f32[24,64,256]{2,1,0:T(8,128)S(1)}, f32[24,64,256]{2,1,0:T(8,128)}, u32[]{:S(2)}) copy-start(f32[24,64,256]{2,1,0:T(8,128)} %grad_ref.1) | copy-start | bytes 4718596
  3.9 0.7 copy-start.2

commit v2 on v1

--- a/solution.py
+++ b/solution.py
@@ -52,6 +52,12 @@
         peer = peer + (mask // bit % 2) * (1 - 2 * (me // bit % 2)) * bit
         bit *= 2
     return peer
+
+
+def nth_mask(s, count):
+    if isinstance(s, int) and s == count - 1:
+        return 0
+    return (1 - s % 2) * (count // 2 + s // 2) + s % 2 * ((s + 1) // 2)
 
 
 def spread_kernel(
@@ -109,7 +115,7 @@
     places = [jnp.int32(0)] * factors
     running = jnp.int32(0)
     for s in range(dp_count):
-        peer = flipped(dp_me, dp_count - 1 - s, dp_count)
+        peer = flipped(dp_me, nth_mask(s, dp_count), dp_count)
         bases[s] = running
         for f in range(factors):
             hit = targets[f] == peer
@@ -161,7 +167,7 @@
             dst_ref=recv_ref.at[dp_me],
             send_sem=out_send.at[s],
             recv_sem=out_recv.at[s],
-            device_id=(flipped(dp_me, dp_count - 1 - s, dp_count), mp_me),
+            device_id=(flipped(dp_me, nth_mask(s, dp_count), dp_count), mp_me),
             device_id_type=MESH,
         )
 
@@ -349,7 +355,7 @@
         compiler_params=pltpu.CompilerParams(
             collective_id=0, has_side_effects=True, vmem_limit_bytes=28 * 2**20
         ),
-    )(root_table, statistics, gradient)
+    )(*(pltpu.with_memory_space_constraint(x, pltpu.HBM) for x in (root_table, statistics, gradient)))
     per_step = 2
     return pl.pallas_call(
         functools.partial(store_kernel, per_peer, per_step),

time: 96.6 us -> 85.2 us (0.88)
  the two profiles are of different devices: /device:TPU:0 before, /device:TPU:8 now
where the time goes in v2:
time: 85.2 us; the launch traced here: 85.1 us
  Pallas kernels  84.4 us (99%)
    pallas_call x1, Pallas kernels, on_device(): pl.pallas_call(functools.partial(spread_kernel, dp_count, mp_count, per_p...  77.6 us
    pallas_call x1, Pallas kernels, on_device(): pl.pallas_call(functools.partial(store_kernel, per_peer, per_step), grid=...  6.83 us

profile of v2, /device:TPU:8, one launch (start us, length us, event | category | flops | bytes accessed | tf_op | source)
XLA Modules:
  0.0 85.1 jit_solution(9240728111203425122)
XLA Ops:
  0.6 77.6 %shard_map.50 = (f32[8,776,128]{2,1,0:T(8,128)S(1)}, f32[24,64,256]{2,1,0:T(8,128)S(1)}, s32[1,24]{1,0:T(1,128)S(1)}) custom-call(s32[1,96]{1,0:T(1,128)} %table_ref.1, f32[12,256,256]{2,1,0:T(8,128)} %stat_ref.1, f32[24,64,256]{2,1,0:T(8,128)} %grad_ref.1), custom_call_target="tpu_custom_call" | custom-call | tf_op jit(solution)/shard_map/pallas_call | solution.py:327
  78.2 6.8 %shard_map.51 = (f32[24,256,256]{2,1,0:T(8,128)}, f32[24,64,256]{2,1,0:T(8,128)}) custom-call(s32[1,24]{1,0:T(1,128)S(1)} %get-tuple-element.5.codes_ref, f32[8,776,128]{2,1,0:T(8,128)S(1)} %get-tuple-element.6.recv_ref, f32[24,64,256]{2,1,0:T(8,128)S(1)} %get-tuple-element.7.back_ref), custom_call_target="tpu_custom_call" | custom-call | tf_op jit(solution)/shard_map/pallas_call | solution.py:360

commit v3 on v2

--- a/solution.py
+++ b/solution.py
@@ -356,7 +356,7 @@
             collective_id=0, has_side_effects=True, vmem_limit_bytes=28 * 2**20
         ),
     )(*(pltpu.with_memory_space_constraint(x, pltpu.HBM) for x in (root_table, statistics, gradient)))
-    per_step = 2
+    per_step = 4
     return pl.pallas_call(
         functools.partial(store_kernel, per_peer, per_step),
         grid=(capacity // per_step,),

time: 85.2 us -> 83.3 us (0.978)
  Pallas kernels: 84.4 us -> 82.5 us
    pallas_call x1, Pallas kernels: 6.83 us -> 4.94 us  [on_device(): pl.pallas_call(functools.partial(store_kernel, per_peer, per_step), grid=...]
where the time goes in v3:
time: 83.3 us; the launch traced here: 83.2 us
  Pallas kernels  82.5 us (99%)
    pallas_call x1, Pallas kernels, on_device(): pl.pallas_call(functools.partial(spread_kernel, dp_count, mp_count, per_p...  77.6 us
    pallas_call x1, Pallas kernels, on_device(): pl.pallas_call(functools.partial(store_kernel, per_peer, per_step), grid=...  4.94 us

profile of v3, /device:TPU:8, one launch (start us, length us, event | category | flops | bytes accessed | tf_op | source)
XLA Modules:
  0.0 83.2 jit_solution(9089288437715916505)
XLA Ops:
  0.6 77.6 %shard_map.50 = (f32[8,776,128]{2,1,0:T(8,128)S(1)}, f32[24,64,256]{2,1,0:T(8,128)S(1)}, s32[1,24]{1,0:T(1,128)S(1)}) custom-call(s32[1,96]{1,0:T(1,128)} %table_ref.1, f32[12,256,256]{2,1,0:T(8,128)} %stat_ref.1, f32[24,64,256]{2,1,0:T(8,128)} %grad_ref.1), custom_call_target="tpu_custom_call" | custom-call | tf_op jit(solution)/shard_map/pallas_call | solution.py:327
  78.2 4.9 %shard_map.51 = (f32[24,256,256]{2,1,0:T(8,128)}, f32[24,64,256]{2,1,0:T(8,128)}) custom-call(s32[1,24]{1,0:T(1,128)S(1)} %get-tuple-element.5.codes_ref, f32[8,776,128]{2,1,0:T(8,128)S(1)} %get-tuple-element.6.recv_ref, f32[24,64,256]{2,1,0:T(8,128)S(1)} %get-tuple-element.7.back_ref), custom_call_target="tpu_custom_call" | custom-call | tf_op jit(solution)/shard_map/pallas_call | solution.py:360
